TPU v7x, 32 devices: a whole 2x2x4 slice. The times are simulated.
32 devices in a mesh: win: 4 (over z), rcv: 8 (over y, x, core).
Axes of the slice: x: 2, y: 2, z: 4, core: 2. Of those that a mesh axis runs over, the one named last changes fastest.
Arguments:
- spectra: bfloat16 [512, 16, 2, 1024], P('rcv', 'win'), may hold values from -6 to 6
- source_block: int32 [1], replicated, may hold values from 0 to 7
Outputs:
- correlations: bfloat16 [512, 64, 2048], P('rcv', None, 'win')
All inputs are finite; a program needn't handle non-finite values.
Results may differ from a plain program's by a relative error of at most 0.015.
Values may be sent and summed in bfloat16 or wider, within the bound.
A program may use at most 256 MiB of HBM per device.

v0:
```python
import math

import jax
import jax.numpy as jnp
from jax import lax
from jax.sharding import PartitionSpec as P


def broadcast(shard, axis, root):
    mine = lax.axis_index(axis) == root
    return lax.psum(jnp.where(mine, shard, jnp.zeros_like(shard)), axis)


def cross_terms(receivers, source):
    flipped = jnp.stack([-receivers[:, :, 1], receivers[:, :, 0]], axis=2)
    real_part = jnp.einsum("rwcf,swcf->rsf", receivers, source, preferred_element_type=jnp.float32)
    imag_part = jnp.einsum("rwcf,swcf->rsf", flipped, source, preferred_element_type=jnp.float32)
    return jnp.stack([real_part, imag_part], axis=2)


def lag_table(n_freqs):
    n_lags = 2 * n_freqs
    freq_index = jnp.arange(n_freqs, dtype=jnp.int32)
    lag_index = jnp.arange(n_lags, dtype=jnp.int32) - n_freqs
    phase_index = freq_index[:, None] * lag_index[None, :] % n_lags
    angle = 2.0 * math.pi / n_lags * phase_index.astype(jnp.float32)
    return jnp.concatenate([jnp.cos(angle), -jnp.sin(angle)], axis=0).astype(jnp.bfloat16)


def to_lags(cross_spec, lag_scale, table):
    row_count, source_count, two_parts, n_freqs = cross_spec.shape
    flat_spec = cross_spec.astype(jnp.bfloat16).reshape(
        row_count * source_count, two_parts * n_freqs
    )
    lagged = jnp.dot(flat_spec, table, preferred_element_type=jnp.float32) * lag_scale
    return lagged.astype(jnp.bfloat16).reshape(row_count, source_count, table.shape[1])


def body(spectra, source_block):
    root_index = source_block[0]
    win_count = lax.axis_size("win")
    n_freqs = spectra.shape[3]
    lag_scale = 1.0 / math.sqrt(2 * n_freqs * spectra.shape[1] * win_count)
    table = lag_table(n_freqs)
    receivers = lax.all_to_all(spectra, "win", split_axis=0, concat_axis=1, tiled=True)
    whole_block = lax.all_gather(spectra, "win", axis=1, tiled=True)
    source = broadcast(whole_block, "rcv", root_index)
    cross_spec = cross_terms(receivers, source)
    lagged = to_lags(cross_spec, lag_scale, table)
    return lax.all_to_all(lagged, "win", split_axis=2, concat_axis=0, tiled=True)


def solution(mesh):
    in_specs = (P("rcv", "win", None, None), P())
    out_specs = P("rcv", None, "win")
    return jax.shard_map(body, mesh=mesh, in_specs=in_specs, out_specs=out_specs, check_vma=False)
```

profile of v0, /device:TPU:0, one launch (start us, length us, event | category | flops | bytes accessed | tf_op | source)
XLA Modules:
  0.0 450.8 jit_solution(3792921551736540989)
XLA Ops:
  6.5 0.0 all-gather.2.cloned.1.call-start
  6.5 2.8 copy.31
  9.3 0.0 all-gather.2.cloned.1.call-update
  9.3 6.4 %all-to-all-start = ((bf16[64,4,2,1024]{3,2,1,0:T(2,128)(2,1)}), bf16[64,4,2,1024]{3,2,1,0:T(2,128)(2,1)S(1)}, u32[]{:S(2)}, u32[]{:S(2)}) async-start(bf16[64,4,2,1024]{3,2,1,0:T(2,128)(2,1)} %param.2), calls=%async_computation | async-start | bytes 2097152 | tf_op jit(solution)/shard_map/all_to_all | solution.py:45
  15.7 0.0 all-reduce.2.cloned.1.call-start
  16.3 93.1 %all-gather.2.cloned.1.call-done = bf16[64,16,2,1024]{3,0,2,1:T(8,128)(2,1)} async-done(((bf16[64,4,2,1024]{3,0,2,1:T(8,128)(2,1)}), bf16[64,16,2,1024]{3,0,2,1:T(8,128)(2,1)}) %all-gather.2.cloned.1.call-update) | async-done | bytes 4194320 | tf_op jit(solution)/shard_map/all_gather | solution.py:46
  109.5 12.9 %copy.32 = bf16[64,16,2,1024]{0,1,2,3:T(8,128)(2,1)} copy(bf16[64,16,2,1024]{3,0,2,1:T(8,128)(2,1)} %all-gather.2.cloned.1.call-done) | data formatting | bytes 8388608 | tf_op jit(solution)/shard_map/all_gather | solution.py:46
  122.4 3.8 broadcast_select_fusion
  126.2 0.0 all-reduce.2.cloned.1.call-update
  126.2 35.0 %cosine_convert_fusion = (bf16[1024,2048]{1,0:T(8,128)(2,1)}, bf16[1024,2048]{1,0:T(8,128)(2,1)}) fusion(s32[2048]{0:T(1024)S(1)} %iota_add_fusion), kind=kLoop, calls=%fused_computation.19 | loop fusion | flops 35651584 | bytes 8396800 | tf_op jit(solution)/shard_map/convert
  161.3 0.0 all-to-all-done
  161.3 0.6 copy.33
  161.9 0.1 copy.34
  162.0 12.2 %copy.35 = bf16[16,16,2,1024]{1,0,2,3:T(8,128)(2,1)} copy(bf16[16,16,2,1024]{3,0,2,1:T(8,128)(2,1)S(1)} %bitcast.42) | data formatting | bytes 2097152 | tf_op jit(solution)/shard_map/all_to_all | solution.py:45
  174.2 6.7 %slice_negate_fusion = (bf16[16,16,1,1024]{1,0,2,3:T(8,128)(2,1)}, bf16[16,16,1,1024]{1,0,2,3:T(8,128)(2,1)}) fusion(bf16[16,16,2,1024]{1,0,2,3:T(8,128)(2,1)} %copy.35), kind=kLoop, calls=%fused_computation.26 | loop fusion | flops 262144 | bytes 2097152 | tf_op jit(solution)/shard_map/neg | solution.py:15
  180.8 73.4 %all-reduce.2.cloned.1.call-done = bf16[64,16,2,1024]{0,1,2,3:T(8,128)(2,1)} async-done(((bf16[64,16,2,1024]{0,1,2,3:T(8,128)(2,1)}), bf16[64,16,2,1024]{0,1,2,3:T(8,128)(2,1)}) %all-reduce.2.cloned.1.call-update) | async-done | bytes 4194320 | tf_op jit(solution)/shard_map/psum | solution.py:11
  254.2 8.2 %fusion.16 = bf16[16,64,1,1024]{1,0,3,2:T(8,128)(2,1)S(1)} fusion(bf16[16,16,2,1024]{1,0,2,3:T(8,128)(2,1)} %copy.35, bf16[64,16,2,1024]{0,1,2,3:T(8,128)(2,1)} %all-reduce.2.cloned.1.call-done), kind=kOutput, calls=%fused_computation.24 | convolution fusion | flops 68157440 | bytes 7340032 | tf_op jit(solution)/shard_map/rwcf,swcf->rsf/dot_general | solution.py:16
  262.4 10.2 %fusion.17 = bf16[16,64,1,1024]{1,0,3,2:T(8,128)(2,1)} fusion(bf16[64,16,2,1024]{0,1,2,3:T(8,128)(2,1)} %all-reduce.2.cloned.1.call-done, bf16[16,16,1,1024]{1,0,2,3:T(8,128)(2,1)} %get-tuple-element.6, bf16[16,16,1,1024]{1,0,2,3:T(8,128)(2,1)} %get-tuple-element.5), kind=kOutput, calls=%fused_computation.25 | convolution fusion | flops 70254592 | bytes 7340032 | tf_op jit(solution)/shard_map/rwcf,swcf->rsf/dot_general | solution.py:17
  272.6 7.3 %pad_maximum_fusion = bf16[16,64,2,1024]{1,0,3,2:T(8,128)(2,1)} fusion(bf16[16,64,1,1024]{1,0,3,2:T(8,128)(2,1)} %fusion.17, bf16[16,64,1,1024]{1,0,3,2:T(8,128)(2,1)S(1)} %fusion.16), kind=kLoop, calls=%fused_computation.10 | loop fusion | flops 2097152 | bytes 8388608 | tf_op jit(solution)/shard_map/stack | solution.py:18
  279.9 11.9 %reshape.13 = bf16[1024,2048]{0,1:T(8,128)(2,1)} reshape(bf16[16,64,2,1024]{1,0,3,2:T(8,128)(2,1)} %pad_maximum_fusion) | data formatting | bytes 8388608 | tf_op jit(solution)/shard_map/convert_element_type | solution.py:32
  291.8 14.0 %multiply_convert_fusion = bf16[1024,2048]{1,0:T(8,128)(2,1)} fusion(bf16[1024,2048]{0,1:T(8,128)(2,1)} %reshape.13, bf16[1024,2048]{1,0:T(8,128)(2,1)} %get-tuple-element.8, bf16[1024,2048]{1,0:T(8,128)(2,1)} %get-tuple-element.7), kind=kOutput, calls=%fused_computation.17 | convolution fusion | flops 8610906112 | bytes 16777216 | tf_op jit(solution)/shard_map/dot_general | solution.py:35
  305.8 10.9 %copy.39 = bf16[16,64,2048]{1,0,2:T(8,128)(2,1)} copy(bf16[16,64,2048]{2,1,0:T(8,128)(2,1)} %bitcast.41) | data formatting | bytes 8388608 | tf_op jit(solution)/shard_map/reshape | solution.py:36
  316.8 9.5 %reshape.14 = bf16[4,2,262144]{2,1,0:T(2,128)(2,1)} reshape(bf16[2048,16,64]{2,1,0:T(8,128)(2,1)} %bitcast.39) | data formatting | bytes 8388608
  326.3 98.6 %all_to_all.36 = bf16[4,2,262144]{2,1,0:T(2,128)(2,1)} all-to-all(bf16[4,2,262144]{2,1,0:T(2,128)(2,1)} %reshape.14), channel_id=1, replica_groups=mesh['win'=4,'rcv'=8] {'win'}, dimensions={0} | all-to-all | bytes 8388608 | tf_op jit(solution)/shard_map/all_to_all | solution.py:50
  424.9 9.3 %reshape.15 = bf16[2048,16,64]{2,1,0:T(8,128)(2,1)} reshape(bf16[4,2,262144]{2,1,0:T(2,128)(2,1)} %all_to_all.36) | data formatting | bytes 8388608
  434.2 9.7 %copy.40 = bf16[4,16,64,512]{3,2,1,0:T(8,128)(2,1)} copy(bf16[4,16,64,512]{2,1,3,0:T(8,128)(2,1)} %bitcast.40) | data formatting | bytes 8388608 | tf_op jit(solution)/shard_map/all_to_all | solution.py:50
  (1 shorter events, 0.0 us)
Async XLA Ops:
  6.5 103.0 %all-gather.2.cloned.1.call-start = ((), (), s32[]{:S(2)}) async-start(), calls=%async_computation.2 | async-start | bytes 5242880 | tf_op jit(solution)/shard_map/all_gather | solution.py:46
  9.3 151.9 %all-to-all-start = ((bf16[64,4,2,1024]{3,2,1,0:T(2,128)(2,1)}), bf16[64,4,2,1024]{3,2,1,0:T(2,128)(2,1)S(1)}, u32[]{:S(2)}, u32[]{:S(2)}) async-start(bf16[64,4,2,1024]{3,2,1,0:T(2,128)(2,1)} %param.2), calls=%async_computation | async-start | bytes 2097152 | tf_op jit(solution)/shard_map/all_to_all | solution.py:45
  15.7 238.5 %all-reduce.2.cloned.1.call-start = ((), (), s32[]{:S(2)}) async-start(), calls=%async_computation.3 | async-start | bytes 16777216 | tf_op jit(solution)/shard_map/psum | solution.py:11
Sparse Core Ops, SparseCore 0:
  9.5 99.9 all-gather.1
  126.3 127.8 all-reduce.1
where the time goes:
time: 452 us; the launch traced here: 451 us
  waiting for transfers between devices  167 us (37%)
  blocking collectives  98.6 us (22%)
  local copies, waits for them, and re-layouts  79.9 us (18%)
  other arithmetic  52.8 us (12%)
  matrix products  32.4 us (7%)
  between operations  14.1 us (3%)
  starting transfers between devices  6.36 us (1%)
    all_to_all x1, blocking collectives, body(): lax.all_to_all(lagged, 'win', split_axis=2, concat_axis=0, tiled=True)  98.6 us
    all_gather x1, waiting for transfers between devices, body(): whole_block = lax.all_gather(spectra, 'win', axis=1, tiled=True)  93.1 us
    psum x1, waiting for transfers between devices, broadcast(): return lax.psum(jnp.where(mine, shard, jnp.zeros_like(shard)), axis)  73.4 us
    another operation x1, other arithmetic  35 us
    unnamed x3, local copies, waits for them, and re-layouts  21.6 us
    dot_general x1, matrix products, to_lags(): jnp.dot(flat_spec, table, preferred_element_type=jnp.float32) * lag_scale  14 us
    all_gather x1, local copies, waits for them, and re-layouts, body(): whole_block = lax.all_gather(spectra, 'win', axis=1, tiled=True)  12.9 us
    all_to_all x3, local copies, waits for them, and re-layouts, body(): lax.all_to_all(spectra, 'win', split_axis=0, concat_axis=1, tiled=True)  12.9 us
  transfers between devices with their start and end apart: 3, of which 2 were waited for; matrix products, arithmetic and copies ran while one was open for 16% of the time, Pallas kernels for 0%

commit v1 on v0

v1 whole, which is shorter than its diff:
```python
import functools
import math

import jax
import jax.numpy as jnp
import ml_dtypes
import numpy as np
from jax import lax
from jax.experimental import pallas as pl
from jax.experimental.pallas import tpu as pltpu
from jax.sharding import PartitionSpec as P

MESH = pl.DeviceIdType.MESH
LANES = 128
CHUNKS = 4


def lag_table(n_freqs, n_win, groups):
    n_lags = 2 * n_freqs
    column = np.arange(n_freqs)
    freq = (column % groups) * LANES + column // groups
    lag = (np.arange(n_lags) - n_freqs).reshape(n_win, 1, n_lags // n_win, 1)
    angle = (2.0 * math.pi / n_lags) * ((freq * lag) % n_lags)
    table = np.concatenate([np.cos(angle), -np.sin(angle)], axis=1)
    return table.astype(ml_dtypes.bfloat16)


def gather_kernel(n_win, n_rcv, root_ref, own_ref, recv_out, src_out, slots, piece_sem, sp_send, sp_recv,
                  r_send, r_recv, z_send, z_recv, x_send, x_recv, c_send, c_recv, local_sem):
    me_w = lax.axis_index("win")
    me_r = lax.axis_index("rcv")
    n_chan, rows = own_ref.shape[0], own_ref.shape[1]
    part = n_chan // n_rcv
    chunk = n_chan // CHUNKS
    sibling = me_r + 1 - 2 * lax.rem(me_r, 2)
    n_chip = n_rcv // 2

    barrier = pltpu.get_barrier_semaphore()

    @pl.when(me_w > 0)
    def _():
        pl.semaphore_signal(barrier, inc=1, device_id=(me_w - 1, me_r), device_id_type=MESH)

    @pl.when(me_w < n_win - 1)
    def _():
        pl.semaphore_signal(barrier, inc=1, device_id=(me_w + 1, me_r), device_id_type=MESH)

    @pl.loop(1, n_rcv)
    def _(d):
        pl.semaphore_signal(barrier, inc=1, device_id=(me_w, lax.rem(me_r + d, n_rcv)), device_id_type=MESH)

    on_line = (me_w > 0).astype(jnp.int32) + (me_w < n_win - 1).astype(jnp.int32)
    pl.semaphore_wait(barrier, n_rcv - 1 + on_line)

    def piece_copy(d):
        target = lax.rem(me_r + d, n_rcv)
        return pltpu.make_async_remote_copy(
            src_ref=own_ref.at[pl.ds(target * part, part)], dst_ref=slots.at[me_r],
            send_sem=sp_send.at[d], recv_sem=sp_recv.at[d],
            device_id=(me_w, target), device_id_type=MESH)

    def hop(buffer, first, count, origin, send_sem, recv_sem, step):
        block = buffer.at[pl.ds(first, count), pl.ds(origin * rows, rows), :]
        return pltpu.make_async_remote_copy(
            src_ref=block, dst_ref=block, send_sem=send_sem, recv_sem=recv_sem,
            device_id=(me_w + step, me_r), device_id_type=MESH)

    def recv_hop(c, t, way):
        step = 1 - 2 * way
        return hop(recv_out, c * chunk, chunk, me_w - step * t, r_send.at[way, t, c], r_recv.at[way, t, c], step)

    def src_hop(t, way):
        step = 1 - 2 * way
        return hop(src_out, me_r * part, part, me_w - step * t, z_send.at[way, t], z_recv.at[way, t], step)

    def can_send(t, way):
        return (me_w >= t) & (me_w < n_win - 1) if way == 0 else (me_w + t < n_win) & (me_w > 0)

    def can_receive(t, way):
        return me_w > t if way == 0 else me_w + t + 1 < n_win


    def recv_arrival(c, t, way):
        step = 1 - 2 * way
        return hop(recv_out, c * chunk, chunk, me_w - step * (t + 1), r_send.at[way, t, c], r_recv.at[way, t, c], 0)

    def src_arrival(t, way):
        step = 1 - 2 * way
        return hop(src_out, me_r * part, part, me_w - step * (t + 1), z_send.at[way, t], z_recv.at[way, t], 0)

    @pl.loop(1, n_rcv)
    def _(d):
        piece_copy(d).start()

    own_local = pltpu.make_async_copy(own_ref, recv_out.at[:, pl.ds(me_w * rows, rows), :], local_sem.at[0])
    own_local.start()
    piece_local = pltpu.make_async_copy(own_ref.at[pl.ds(me_r * part, part)], slots.at[me_r], local_sem.at[1])
    piece_local.start()
    own_local.wait()

    def start_own(c):
        for way in range(2):
            @pl.when(can_send(0, way))
            def _():
                recv_hop(c, 0, way).start()

    for c in range(CHUNKS):
        start_own(c)

    piece_local.wait()

    @pl.loop(1, n_rcv)
    def _(d):
        piece_copy(d).wait()

    piece_sem[...] = slots[root_ref[0]]
    mine = src_out.at[pl.ds(me_r * part, part), pl.ds(me_w * rows, rows), :]
    placed = pltpu.make_async_copy(piece_sem, mine, local_sem.at[2])
    placed.start()
    placed.wait()
    for way in range(2):
        @pl.when(can_send(0, way))
        def _():
            src_hop(0, way).start()
    for t in range(n_win - 1):
        for way in range(2):
            @pl.when(can_receive(t, way))
            def _():
                src_arrival(t, way).wait_recv()

            @pl.when(can_send(t + 1, way))
            def _():
                src_hop(t + 1, way).start()

    def block_copy(owner, target, send_sem, recv_sem):
        block = src_out.at[pl.ds(owner * part, part)]
        return pltpu.make_async_remote_copy(
            src_ref=block, dst_ref=block, send_sem=send_sem, recv_sem=recv_sem,
            device_id=(me_w, target), device_id_type=MESH)

    def chip_copy(d):
        return block_copy(me_r, lax.rem(me_r + 2 * d, n_rcv), x_send.at[d], x_recv.at[d])

    def core_copy(d):
        return block_copy(lax.rem(me_r - 2 * d + n_rcv, n_rcv), sibling, c_send.at[d], c_recv.at[d])

    def core_arrival(d):
        return block_copy(lax.rem(sibling - 2 * d + n_rcv, n_rcv), sibling, c_send.at[d], c_recv.at[d])

    def chip_arrival(d):
        return block_copy(lax.rem(me_r - 2 * d + n_rcv, n_rcv), sibling, x_send.at[d], x_recv.at[d])

    @pl.loop(1, n_chip)
    def _(d):
        chip_copy(d).start()

    core_copy(0).start()

    for c in range(CHUNKS):
        for t in range(n_win - 1):
            for way in range(2):
                @pl.when(can_receive(t, way))
                def _():
                    recv_arrival(c, t, way).wait_recv()

                @pl.when(can_send(t + 1, way))
                def _():
                    recv_hop(c, t + 1, way).start()

    @pl.loop(1, n_chip)
    def _(d):
        chip_arrival(d).wait_recv()
        core_copy(d).start()

    @pl.loop(0, n_chip)
    def _(d):
        core_arrival(d).wait_recv()
        core_copy(d).wait_send()

    @pl.loop(1, n_chip)
    def _(d):
        chip_copy(d).wait_send()

    for t in range(n_win - 1):
        for way in range(2):
            @pl.when(can_send(t, way))
            def _():
                src_hop(t, way).wait_send()
                for c in range(CHUNKS):
                    recv_hop(c, t, way).wait_send()


def gather(root, own, n_win, n_rcv):
    n_chan, rows, lanes = own.shape
    part = n_chan // n_rcv
    whole = jax.ShapeDtypeStruct((n_chan, n_win * rows, lanes), own.dtype)
    sem = pltpu.SemaphoreType.DMA
    return pl.pallas_call(
        functools.partial(gather_kernel, n_win, n_rcv),
        out_shape=(whole, whole),
        in_specs=[pl.BlockSpec(memory_space=pltpu.SMEM), pl.BlockSpec(memory_space=pl.ANY)],
        out_specs=(pl.BlockSpec(memory_space=pl.ANY), pl.BlockSpec(memory_space=pl.ANY)),
        scratch_shapes=[
            pltpu.VMEM((n_rcv, part, rows, lanes), own.dtype),
            pltpu.VMEM((part, rows, lanes), own.dtype),
            sem((n_rcv,)), sem((n_rcv,)),
            sem((2, n_win, CHUNKS)), sem((2, n_win, CHUNKS)),
            sem((2, n_win)), sem((2, n_win)),
            sem((n_rcv,)), sem((n_rcv,)),
            sem((n_rcv,)), sem((n_rcv,)),
            sem((3,)),
        ],
        compiler_params=pltpu.CompilerParams(
            collective_id=0, has_side_effects=True, vmem_limit_bytes=16 << 20),
        name="gather",
    )(root, own)


def store_turned(flipped, row, block):
    turned = block.astype(jnp.float32).T
    at = pl.ds(pl.multiple_of(row * LANES, LANES), LANES)
    for slab in range(flipped.shape[0]):
        flipped[slab, at, :] = turned[:, slab * LANES:(slab + 1) * LANES]


def load_turned(flipped, j, count):
    slabs = [flipped[slab, pl.ds(j, count, stride=LANES), :] for slab in range(flipped.shape[0])]
    return jnp.concatenate(slabs, axis=1)


def correlate_kernel(lag_scale, groups, r_ref, s_ref, table_ref, out_ref, flipped, weights, x_real, x_imag):
    n_src, depth, lanes = s_ref.shape
    n_chan = r_ref.shape[0]
    n_lags = table_ref.shape[1]
    lane = lax.broadcasted_iota(jnp.int32, (1, depth), 1)

    @pl.when(pl.program_id(0) == 0)
    def _():
        @pl.loop(0, n_src)
        def _(s):
            store_turned(flipped, s, s_ref[s])

        is_real = lax.rem(lane, 2 * groups) < groups

        @pl.loop(0, lanes)
        def _(j):
            spec = load_turned(flipped, j, n_src)
            turned = jnp.where(is_real, pltpu.roll(spec, depth - groups, 1), -pltpu.roll(spec, groups, 1))
            weights[j, :n_src, :] = spec.astype(jnp.bfloat16)
            weights[j, n_src:, :] = turned.astype(jnp.bfloat16)

    @pl.loop(0, n_chan)
    def _(r):
        store_turned(flipped, r, r_ref[r])

    row = lax.broadcasted_iota(jnp.int32, (groups, depth), 0)
    picked = (lax.rem(lax.broadcasted_iota(jnp.int32, (groups, depth), 1), groups) == row)[None]
    first_half = lax.broadcasted_iota(jnp.int32, (1, 1, 2 * n_src), 2) < n_src

    @pl.loop(0, lanes // 2)
    def _(jp):
        reals, imags = [], []
        for k in range(2):
            j = 2 * jp + k
            spec = load_turned(flipped, j, n_chan)
            spread = jnp.where(picked, spec[:, None, :], 0.0).reshape(n_chan * groups, depth).astype(jnp.bfloat16)
            real = weights[j, :n_src, :]
            imag = weights[j, n_src:, :]
            both = jnp.concatenate([real, real, imag, imag], axis=0)
            cross = lax.dot_general(spread, both, (((1,), (1,)), ((), ())), preferred_element_type=jnp.float32)
            for half, kept in ((0, reals), (1, imags)):
                part = cross[:, half * 2 * n_src:(half + 1) * 2 * n_src].reshape(n_chan // 2, 2, groups, 2 * n_src)
                kept.append(jnp.where(first_half, part[:, 0], part[:, 1]))
        at = pl.ds(pl.multiple_of(jp * 2 * groups, 2 * groups), 2 * groups)
        x_real[:, at, :] = jnp.concatenate(reals, axis=1).astype(jnp.bfloat16)
        x_imag[:, at, :] = jnp.concatenate(imags, axis=1).astype(jnp.bfloat16)

    @pl.loop(0, n_chan // 4)
    def _(q):
        real = jnp.concatenate([x_real[2 * q], x_real[2 * q + 1]], axis=1)
        imag = jnp.concatenate([x_imag[2 * q], x_imag[2 * q + 1]], axis=1)
        lagged = jnp.dot(table_ref[0], real, preferred_element_type=jnp.float32)
        lagged += jnp.dot(table_ref[1], imag, preferred_element_type=jnp.float32)
        turned = (lagged * lag_scale).T.astype(jnp.bfloat16)
        out_ref[pl.ds(q * 4, 4)] = turned.reshape(4, n_src, n_lags)


def correlate(receivers, source, table, lag_scale, groups):
    n_chan, depth, lanes = receivers.shape
    n_src = source.shape[0]
    n_lags, n_freqs = table.shape[1:]
    chunk = n_chan // CHUNKS
    bf16 = jnp.bfloat16
    return pl.pallas_call(
        functools.partial(correlate_kernel, lag_scale, groups),
        grid=(CHUNKS,),
        out_shape=jax.ShapeDtypeStruct((n_chan, n_src, n_lags), bf16),
        in_specs=[
            pl.BlockSpec((chunk, depth, lanes), lambda c: (c, 0, 0)),
            pl.BlockSpec((n_src, depth, lanes), lambda c: (0, 0, 0)),
            pl.BlockSpec((2, n_lags, n_freqs), lambda c: (0, 0, 0)),
        ],
        out_specs=pl.BlockSpec((chunk, n_src, n_lags), lambda c: (c, 0, 0)),
        scratch_shapes=[
            pltpu.VMEM((depth // LANES, n_src * lanes, LANES), jnp.float32),
            pltpu.VMEM((lanes, 2 * n_src, depth), bf16),
            pltpu.VMEM((chunk // 2, n_freqs, 2 * n_src), bf16),
            pltpu.VMEM((chunk // 2, n_freqs, 2 * n_src), bf16),
        ],
        compiler_params=pltpu.CompilerParams(vmem_limit_bytes=56 << 20),
        name="correlate",
    )(receivers, source, table)


def body(n_win, n_rcv, spectra, source_block):
    n_chan, n_time, parts, n_freqs = spectra.shape
    groups = n_freqs // LANES
    lag_scale = 1.0 / math.sqrt(2 * n_freqs * n_time * n_win)
    tables = jnp.asarray(lag_table(n_freqs, n_win, groups))
    table = lax.dynamic_index_in_dim(tables, lax.axis_index("win"), 0, keepdims=False)
    own = spectra.reshape(n_chan, n_time * parts * groups, LANES)
    receivers, source = gather(source_block, own, n_win, n_rcv)
    return correlate(receivers, source, table, lag_scale, groups)


def solution(mesh):
    in_specs = (P("rcv", "win", None, None), P())
    out_specs = P("rcv", None, "win")
    fn = functools.partial(body, mesh.shape["win"], mesh.shape["rcv"])
    return jax.shard_map(fn, mesh=mesh, in_specs=in_specs, out_specs=out_specs, check_vma=False)
```

time: 452 us -> 208 us (0.46)
  Pallas kernels: 0 us -> 198 us
  waiting for transfers between devices: 167 us -> 0 us
  blocking collectives: 98.6 us -> 0 us
  local copies, waits for them, and re-layouts: 79.9 us -> 8.78 us
  other arithmetic: 52.8 us -> 0 us
  matrix products: 32.4 us -> 0 us
  between operations: 14.1 us -> 0.68 us
  starting transfers between devices: 6.36 us -> 0 us
    pallas_call x0 -> x2, Pallas kernels: none -> 198 us  [the longest x1 108 us: correlate(): pl.pallas_call(functools.partial(correlate_kernel, lag_scale, groups), gr...]
    all_to_all x1 -> x0, blocking collectives: 98.6 us -> none  [body(): lax.all_to_all(lagged, 'win', split_axis=2, concat_axis=0, tiled=True)]
    all_gather x1 -> x0, waiting for transfers between devices: 93.1 us -> none  [body(): whole_block = lax.all_gather(spectra, 'win', axis=1, tiled=True)]
    psum x1 -> x0, waiting for transfers between devices: 73.4 us -> none  [broadcast(): return lax.psum(jnp.where(mine, shard, jnp.zeros_like(shard)), axis)]
    another operation x2 -> x0, other arithmetic: 42.3 us -> none
    dot_general x3 -> x0, matrix products: 32.4 us -> none  [the longest x1 14 us: to_lags(): jnp.dot(flat_spec, table, preferred_element_type=jnp.float32) * lag_scale]
    all_to_all x4 -> x0, local copies, waits for them, and re-layouts: 22.6 us -> none  [the longest x3 12.9 us: body(): lax.all_to_all(spectra, 'win', split_axis=0, concat_axis=1, tiled=True)]
    unnamed x3 -> x4, local copies, waits for them, and re-layouts: 21.6 us -> 3.9 us
  transfers between devices with their start and end apart: 3 -> 0, of which waited for: 2 -> 0; matrix products, arithmetic and copies ran while one was open for 16% -> 0% of each run, Pallas kernels for 0% -> 0%
where the time goes in v1:
time: 208 us; the launch traced here: 207 us
  Pallas kernels  198 us (95%)
  local copies, waits for them, and re-layouts  8.78 us (4%)
    pallas_call x1, Pallas kernels, correlate(): pl.pallas_call(functools.partial(correlate_kernel, lag_scale, groups), gr...  108 us
    pallas_call x1, Pallas kernels, gather(): pl.pallas_call(functools.partial(gather_kernel, n_win, n_rcv), out_shape=...  90.4 us

profile of v1, /device:TPU:0, one launch (start us, length us, event | category | flops | bytes accessed | tf_op | source)
XLA Modules:
  0.0 207.5 jit_solution(4414465695600009195)
XLA Ops:
  0.7 1.7 reshape.3.own_ref
  2.4 3.1 %dynamic-slice_bitcast_fusion.table_ref = bf16[2,512,1024]{2,1,0:T(8,128)(2,1)} fusion(bf16[4,2,512,1024]{3,2,1,0:T(8,128)(2,1)} %constant.13.clone, s32[]{:T(128)S(6)} %select_n.4), kind=kLoop, calls=%fused_computation | loop fusion | bytes 4194308 | tf_op jit(solution)/shard_map/jit(dynamic_index_in_dim)/squeeze | solution.py:320
  5.5 90.4 %gather.1 = (bf16[64,256,128]{2,1,0:T(8,128)(2,1)S(1)}, bf16[64,256,128]{2,1,0:T(8,128)(2,1)S(1)}) custom-call(s32[1]{0:T(128)S(6)} %copy.4.root_ref, bf16[64,64,128]{2,1,0:T(8,128)(2,1)S(1)} %reshape.3.own_ref), custom_call_target="tpu_custom_call" | custom-call | tf_op jit(solution)/shard_map/gather/pallas_call | solution.py:198
  96.0 0.0 copy-start
  96.0 1.9 copy-done
  97.9 0.0 copy-start.1
  97.9 2.0 copy-done.1
  99.9 107.6 %correlate.1 = bf16[64,64,512]{2,1,0:T(8,128)(2,1)} custom-call(bf16[64,256,128]{2,1,0:T(8,128)(2,1)} %copy-done, bf16[64,256,128]{2,1,0:T(8,128)(2,1)} %copy-done.1, bf16[2,512,1024]{2,1,0:T(8,128)(2,1)} %dynamic-slice_bitcast_fusion.table_ref), custom_call_target="tpu_custom_call" | custom-call | tf_op jit(solution)/shard_map/correlate/pallas_call | solution.py:294
Async XLA Ops:
  96.0 1.9 copy-start
  97.9 2.0 copy-start.1

commit v2 on v1

v2 whole, which is shorter than its diff:
```python
import functools
import math

import jax
import jax.numpy as jnp
import ml_dtypes
import numpy as np
from jax import lax
from jax.experimental import pallas as pl
from jax.experimental.pallas import tpu as pltpu
from jax.sharding import PartitionSpec as P

MESH = pl.DeviceIdType.MESH
LANES = 128
CHUNKS = 4


def lag_table(n_freqs, n_win, groups):
    n_lags = 2 * n_freqs
    column = np.arange(n_freqs)
    freq = (column % groups) * LANES + column // groups
    lag = (np.arange(n_lags) - n_freqs).reshape(n_win, 1, n_lags // n_win, 1)
    angle = (2.0 * math.pi / n_lags) * ((freq * lag) % n_lags)
    table = np.concatenate([np.cos(angle), -np.sin(angle)], axis=1)
    return table.astype(ml_dtypes.bfloat16)


def store_turned(flipped, row, block):
    turned = block.astype(jnp.float32).T
    at = pl.ds(pl.multiple_of(row * LANES, LANES), LANES)
    for slab in range(flipped.shape[0]):
        flipped[slab, at, :] = turned[:, slab * LANES:(slab + 1) * LANES]


def load_turned(flipped, j, count):
    slabs = [flipped[slab, pl.ds(j, count, stride=LANES), :] for slab in range(flipped.shape[0])]
    return jnp.concatenate(slabs, axis=1)


def prepare_source(groups, s_ref, flipped, weights):
    n_src, depth, _ = s_ref.shape

    @pl.loop(0, n_src)
    def _(s):
        store_turned(flipped, s, s_ref[s])

    lane = lax.broadcasted_iota(jnp.int32, (1, depth), 1)
    is_real = lax.rem(lane, 2 * groups) < groups

    @pl.loop(0, LANES)
    def _(j):
        spec = load_turned(flipped, j, n_src)
        turned = jnp.where(is_real, pltpu.roll(spec, depth - groups, 1), -pltpu.roll(spec, groups, 1))
        weights[j, :, :2 * n_src] = jnp.concatenate([spec, spec], axis=0).T.astype(jnp.bfloat16)
        weights[j, :, 2 * n_src:] = jnp.concatenate([turned, turned], axis=0).T.astype(jnp.bfloat16)


def turn_receivers(first, count, r_ref, flipped):
    @pl.loop(0, count)
    def _(r):
        store_turned(flipped, r, r_ref[first + r])


def cross_part(first, last, groups, n_chan, flipped, weights, x_real, x_imag):
    depth, n_src = weights.shape[1], weights.shape[2] // 4
    row = lax.broadcasted_iota(jnp.int32, (groups, depth), 0)
    picked = (lax.rem(lax.broadcasted_iota(jnp.int32, (groups, depth), 1), groups) == row)[None]
    first_half = lax.broadcasted_iota(jnp.int32, (1, 1, 2 * n_src), 2) < n_src

    @pl.loop(first, last)
    def _(jp):
        reals, imags = [], []
        for k in range(2):
            j = 2 * jp + k
            spec = load_turned(flipped, j, n_chan)
            spread = jnp.where(picked, spec[:, None, :], 0.0).reshape(n_chan * groups, depth).astype(jnp.bfloat16)
            cross = jnp.dot(spread, weights[j], preferred_element_type=jnp.float32)
            for half, kept in ((0, reals), (1, imags)):
                part = cross[:, half * 2 * n_src:(half + 1) * 2 * n_src].reshape(n_chan // 2, 2, groups, 2 * n_src)
                kept.append(jnp.where(first_half, part[:, 0], part[:, 1]))
        at = pl.ds(pl.multiple_of(jp * 2 * groups, 2 * groups), 2 * groups)
        x_real[:, at, :] = jnp.concatenate(reals, axis=1).astype(jnp.bfloat16)
        x_imag[:, at, :] = jnp.concatenate(imags, axis=1).astype(jnp.bfloat16)


def lags_of(first, n_chan, lag_scale, table_ref, x_real, x_imag, out_ref):
    n_src, n_lags = out_ref.shape[1:]

    @pl.loop(0, n_chan // 4)
    def _(q):
        real = jnp.concatenate([x_real[2 * q], x_real[2 * q + 1]], axis=1)
        imag = jnp.concatenate([x_imag[2 * q], x_imag[2 * q + 1]], axis=1)
        lagged = jnp.dot(table_ref[0], real, preferred_element_type=jnp.float32)
        lagged += jnp.dot(table_ref[1], imag, preferred_element_type=jnp.float32)
        turned = (lagged * lag_scale).T.astype(jnp.bfloat16)
        out_ref[pl.ds(first + q * 4, 4)] = turned.reshape(4, n_src, n_lags)


def fused_kernel(n_win, n_rcv, groups, lag_scale, root_ref, own_ref, table_ref, out_ref, recv_out, src_out, slots,
                 flipped, weights, x_real, x_imag, sp_send, sp_recv, r_send, r_recv, z_send, z_recv, x_send, x_recv,
                 c_send, c_recv, local_sem):
    me_w = lax.axis_index("win")
    me_r = lax.axis_index("rcv")
    n_chan, rows = own_ref.shape[0], own_ref.shape[1]
    part = n_chan // n_rcv
    chunk = n_chan // CHUNKS
    sibling = me_r + 1 - 2 * lax.rem(me_r, 2)
    n_chip = n_rcv // 2

    barrier = pltpu.get_barrier_semaphore()

    @pl.when(me_w > 0)
    def _():
        pl.semaphore_signal(barrier, inc=1, device_id=(me_w - 1, me_r), device_id_type=MESH)

    @pl.when(me_w < n_win - 1)
    def _():
        pl.semaphore_signal(barrier, inc=1, device_id=(me_w + 1, me_r), device_id_type=MESH)

    @pl.loop(1, n_rcv)
    def _(d):
        pl.semaphore_signal(barrier, inc=1, device_id=(me_w, lax.rem(me_r + d, n_rcv)), device_id_type=MESH)

    on_line = (me_w > 0).astype(jnp.int32) + (me_w < n_win - 1).astype(jnp.int32)
    pl.semaphore_wait(barrier, n_rcv - 1 + on_line)

    def piece_copy(d):
        target = lax.rem(me_r + d, n_rcv)
        return pltpu.make_async_remote_copy(
            src_ref=own_ref.at[pl.ds(target * part, part)], dst_ref=slots.at[me_r],
            send_sem=sp_send.at[d], recv_sem=sp_recv.at[d],
            device_id=(me_w, target), device_id_type=MESH)

    def hop(buffer, first, count, origin, send_sem, recv_sem, step):
        block = buffer.at[pl.ds(first, count), pl.ds(origin * rows, rows), :]
        return pltpu.make_async_remote_copy(
            src_ref=block, dst_ref=block, send_sem=send_sem, recv_sem=recv_sem,
            device_id=(me_w + step, me_r), device_id_type=MESH)

    def recv_hop(c, t, way):
        step = 1 - 2 * way
        return hop(recv_out, c * chunk, chunk, me_w - step * t, r_send.at[way, t, c], r_recv.at[way, t, c], step)

    def src_hop(t, way):
        step = 1 - 2 * way
        return hop(src_out, me_r * part, part, me_w - step * t, z_send.at[way, t], z_recv.at[way, t], step)

    def can_send(t, way):
        return (me_w >= t) & (me_w < n_win - 1) if way == 0 else (me_w + t < n_win) & (me_w > 0)

    def can_receive(t, way):
        return me_w > t if way == 0 else me_w + t + 1 < n_win


    def recv_arrival(c, t, way):
        step = 1 - 2 * way
        return hop(recv_out, c * chunk, chunk, me_w - step * (t + 1), r_send.at[way, t, c], r_recv.at[way, t, c], 0)

    def src_arrival(t, way):
        step = 1 - 2 * way
        return hop(src_out, me_r * part, part, me_w - step * (t + 1), z_send.at[way, t], z_recv.at[way, t], 0)

    @pl.loop(1, n_rcv)
    def _(d):
        piece_copy(d).start()

    own_local = pltpu.make_async_copy(own_ref, recv_out.at[:, pl.ds(me_w * rows, rows), :], local_sem.at[0])
    own_local.start()
    piece_local = pltpu.make_async_copy(own_ref.at[pl.ds(me_r * part, part)], slots.at[me_r], local_sem.at[1])
    piece_local.start()
    own_local.wait()

    def start_own(c):
        for way in range(2):
            @pl.when(can_send(0, way))
            def _():
                recv_hop(c, 0, way).start()

    start_own(0)
    start_own(1)

    piece_local.wait()

    @pl.loop(1, n_rcv)
    def _(d):
        piece_copy(d).wait()

    mine = (pl.ds(me_r * part, part), pl.ds(pl.multiple_of(me_w * rows, rows), rows), slice(None))
    src_out[mine] = slots[root_ref[0]]
    for way in range(2):
        @pl.when(can_send(0, way))
        def _():
            src_hop(0, way).start()
    for c in range(2, CHUNKS):
        start_own(c)
    for t in range(n_win - 1):
        for way in range(2):
            @pl.when(can_receive(t, way))
            def _():
                src_arrival(t, way).wait_recv()

            @pl.when(can_send(t + 1, way))
            def _():
                src_hop(t + 1, way).start()

    def block_copy(owner, target, send_sem, recv_sem):
        block = src_out.at[pl.ds(owner * part, part)]
        return pltpu.make_async_remote_copy(
            src_ref=block, dst_ref=block, send_sem=send_sem, recv_sem=recv_sem,
            device_id=(me_w, target), device_id_type=MESH)

    def chip_copy(d):
        return block_copy(me_r, lax.rem(me_r + 2 * d, n_rcv), x_send.at[d], x_recv.at[d])

    def core_copy(d):
        return block_copy(lax.rem(me_r - 2 * d + n_rcv, n_rcv), sibling, c_send.at[d], c_recv.at[d])

    def core_arrival(d):
        return block_copy(lax.rem(sibling - 2 * d + n_rcv, n_rcv), sibling, c_send.at[d], c_recv.at[d])

    def chip_arrival(d):
        return block_copy(lax.rem(me_r - 2 * d + n_rcv, n_rcv), sibling, x_send.at[d], x_recv.at[d])

    @pl.loop(1, n_chip)
    def _(d):
        chip_copy(d).start()

    core_copy(0).start()

    def forward(c, t):
        for way in range(2):
            @pl.when(can_receive(t, way))
            def _():
                recv_arrival(c, t, way).wait_recv()

            @pl.when(can_send(t + 1, way))
            def _():
                recv_hop(c, t + 1, way).start()

    for t in range(n_win - 1):
        forward(0, t)

    @pl.loop(1, n_chip)
    def _(d):
        chip_arrival(d).wait_recv()
        core_copy(d).start()

    forward(1, 0)

    @pl.loop(0, n_chip)
    def _(d):
        core_arrival(d).wait_recv()

    prepare_source(groups, src_out, flipped, weights)

    pairs = LANES // 2
    cuts = [pairs * t // n_win for t in range(n_win + 1)]

    def compute(c, ahead):
        turn_receivers(c * chunk, chunk, recv_out, flipped)
        for t in range(n_win):
            cross_part(cuts[t], cuts[t + 1], groups, chunk, flipped, weights, x_real, x_imag)
            if ahead and t < n_win - 1:
                forward(c + 1, t)
        lags_of(c * chunk, chunk, lag_scale, table_ref, x_real, x_imag, out_ref)

    def compute_first():
        turn_receivers(0, chunk, recv_out, flipped)
        for t in range(n_win):
            cross_part(cuts[t], cuts[t + 1], groups, chunk, flipped, weights, x_real, x_imag)
            if 0 < t < n_win - 1:
                forward(1, t)
        lags_of(0, chunk, lag_scale, table_ref, x_real, x_imag, out_ref)

    compute_first()

    @pl.loop(1, CHUNKS - 1)
    def _(c):
        compute(c, True)

    compute(CHUNKS - 1, False)

    @pl.loop(0, n_chip)
    def _(d):
        core_copy(d).wait_send()

    @pl.loop(1, n_chip)
    def _(d):
        chip_copy(d).wait_send()

    for t in range(n_win - 1):
        for way in range(2):
            @pl.when(can_send(t, way))
            def _():
                src_hop(t, way).wait_send()
                for c in range(CHUNKS):
                    recv_hop(c, t, way).wait_send()


def fused(root, own, table, n_win, n_rcv, lag_scale, groups):
    n_chan, rows, lanes = own.shape
    part = n_chan // n_rcv
    chunk = n_chan // CHUNKS
    depth = n_win * rows
    n_lags, n_freqs = table.shape[1:]
    bf16 = own.dtype
    sem = pltpu.SemaphoreType.DMA
    return pl.pallas_call(
        functools.partial(fused_kernel, n_win, n_rcv, groups, lag_scale),
        out_shape=jax.ShapeDtypeStruct((n_chan, n_chan, n_lags), bf16),
        in_specs=[
            pl.BlockSpec(memory_space=pltpu.SMEM),
            pl.BlockSpec(memory_space=pl.ANY),
            pl.BlockSpec(memory_space=pltpu.VMEM),
        ],
        out_specs=pl.BlockSpec(memory_space=pltpu.VMEM),
        scratch_shapes=[
            pltpu.VMEM((n_chan, depth, lanes), bf16),
            pltpu.VMEM((n_chan, depth, lanes), bf16),
            pltpu.VMEM((n_rcv, part, rows, lanes), bf16),
            pltpu.VMEM((depth // LANES, n_chan * lanes, LANES), jnp.float32),
            pltpu.VMEM((lanes, depth, 4 * n_chan), bf16),
            pltpu.VMEM((chunk // 2, n_freqs, 2 * n_chan), bf16),
            pltpu.VMEM((chunk // 2, n_freqs, 2 * n_chan), bf16),
            sem((n_rcv,)), sem((n_rcv,)),
            sem((2, n_win, CHUNKS)), sem((2, n_win, CHUNKS)),
            sem((2, n_win)), sem((2, n_win)),
            sem((n_rcv,)), sem((n_rcv,)),
            sem((n_rcv,)), sem((n_rcv,)),
            sem((2,)),
        ],
        compiler_params=pltpu.CompilerParams(
            collective_id=0, has_side_effects=True, vmem_limit_bytes=56 << 20),
        name="fused",
    )(root, own, table)


def body(n_win, n_rcv, spectra, source_block):
    n_chan, n_time, parts, n_freqs = spectra.shape
    groups = n_freqs // LANES
    lag_scale = 1.0 / math.sqrt(2 * n_freqs * n_time * n_win)
    tables = jnp.asarray(lag_table(n_freqs, n_win, groups))
    table = lax.dynamic_index_in_dim(tables, lax.axis_index("win"), 0, keepdims=False)
    own = spectra.reshape(n_chan, n_time * parts * groups, LANES)
    return fused(source_block, own, table, n_win, n_rcv, lag_scale, groups)


def solution(mesh):
    in_specs = (P("rcv", "win", None, None), P())
    out_specs = P("rcv", None, "win")
    fn = functools.partial(body, mesh.shape["win"], mesh.shape["rcv"])
    return jax.shard_map(fn, mesh=mesh, in_specs=in_specs, out_specs=out_specs, check_vma=False)
```

time: 208 us -> 198 us (0.952)
  Pallas kernels: 198 us -> 187 us
    pallas_call x2 -> x1, Pallas kernels: 198 us -> 187 us  [fused(): pl.pallas_call(functools.partial(fused_kernel, n_win, n_rcv, groups, lag_...]
    unnamed x4 -> x1, local copies, waits for them, and re-layouts: 3.9 us -> 4.7 us
where the time goes in v2:
time: 198 us
  Pallas kernels  187 us (94%)
  local copies, waits for them, and re-layouts  10.3 us (5%)
    pallas_call x1, Pallas kernels, fused(): pl.pallas_call(functools.partial(fused_kernel, n_win, n_rcv, groups, lag_...  187 us
    unnamed x1, local copies, waits for them, and re-layouts  4.7 us

profile of v2, /device:TPU:0, one launch (start us, length us, event | category | flops | bytes accessed | tf_op | source)
XLA Modules:
  0.0 197.8 jit_solution(13613302152064997742)
XLA Ops:
  0.7 2.5 %reshape.3.own_ref = bf16[64,64,128]{2,1,0:T(8,128)(2,1)} reshape(bf16[64,4,2,1024]{3,2,1,0:T(2,128)(2,1)} %param.3) | data formatting | bytes 2097152 | tf_op jit(solution)/shard_map/reshape | solution.py:344
  3.2 3.1 %dynamic-slice_bitcast_fusion.table_ref = bf16[2,512,1024]{2,1,0:T(8,128)(2,1)} fusion(bf16[4,2,512,1024]{3,2,1,0:T(8,128)(2,1)} %constant.13.clone, s32[]{:T(128)S(6)} %select_n.4), kind=kLoop, calls=%fused_computation | loop fusion | bytes 4194308 | tf_op jit(solution)/shard_map/jit(dynamic_index_in_dim)/squeeze | solution.py:343
  6.3 186.8 %fused.1 = bf16[64,64,512]{2,1,0:T(8,128)(2,1)} custom-call(s32[1]{0:T(128)S(6)} %copy.5.root_ref, bf16[64,64,128]{2,1,0:T(8,128)(2,1)} %reshape.3.own_ref, bf16[2,512,1024]{2,1,0:T(8,128)(2,1)} %dynamic-slice_bitcast_fusion.table_ref), custom_call_target="tpu_custom_call" | custom-call | tf_op jit(solution)/shard_map/fused/pallas_call | solution.py:308
  193.1 4.7 %copy.6 = bf16[64,64,512]{2,1,0:T(8,128)(2,1)} copy(bf16[64,64,512]{2,1,0:T(8,128)(2,1)} %fused.1) | data formatting | bytes 8388608

commit v3 on v2

--- a/solution.py
+++ b/solution.py
@@ -44,15 +44,18 @@
     def _(s):
         store_turned(flipped, s, s_ref[s])
 
-    lane = lax.broadcasted_iota(jnp.int32, (1, depth), 1)
-    is_real = lax.rem(lane, 2 * groups) < groups
-
-    @pl.loop(0, LANES)
-    def _(j):
-        spec = load_turned(flipped, j, n_src)
-        turned = jnp.where(is_real, pltpu.roll(spec, depth - groups, 1), -pltpu.roll(spec, groups, 1))
-        weights[j, :, :2 * n_src] = jnp.concatenate([spec, spec], axis=0).T.astype(jnp.bfloat16)
-        weights[j, :, 2 * n_src:] = jnp.concatenate([turned, turned], axis=0).T.astype(jnp.bfloat16)
+    first_half = lax.broadcasted_iota(jnp.int32, (1, 2 * n_src), 1) < n_src
+
+    @pl.loop(0, LANES // 2)
+    def _(jp):
+        both = jnp.concatenate([load_turned(flipped, 2 * jp, n_src), load_turned(flipped, 2 * jp + 1, n_src)], axis=0).T
+        crossed = pltpu.roll(both, n_src, 1)
+        for k, (low, high) in enumerate(((both, crossed), (crossed, both))):
+            real = jnp.where(first_half, low, high)
+            pairs = real.reshape(depth // (2 * groups), 2, groups, 2 * n_src)
+            imag = jnp.stack([pairs[:, 1], -pairs[:, 0]], axis=1).reshape(depth, 2 * n_src)
+            weights[2 * jp + k, :, :2 * n_src] = real.astype(jnp.bfloat16)
+            weights[2 * jp + k, :, 2 * n_src:] = imag.astype(jnp.bfloat16)
 
 
 def turn_receivers(first, count, r_ref, flipped):
@@ -63,8 +66,8 @@
 
 def cross_part(first, last, groups, n_chan, flipped, weights, x_real, x_imag):
     depth, n_src = weights.shape[1], weights.shape[2] // 4
-    row = lax.broadcasted_iota(jnp.int32, (groups, depth), 0)
-    picked = (lax.rem(lax.broadcasted_iota(jnp.int32, (groups, depth), 1), groups) == row)[None]
+    row = lax.broadcasted_iota(jnp.int32, (groups, LANES), 0)
+    picked = lax.rem(lax.broadcasted_iota(jnp.int32, (groups, LANES), 1), groups) == row
     first_half = lax.broadcasted_iota(jnp.int32, (1, 1, 2 * n_src), 2) < n_src
 
     @pl.loop(first, last)
@@ -72,8 +75,11 @@
         reals, imags = [], []
         for k in range(2):
             j = 2 * jp + k
-            spec = load_turned(flipped, j, n_chan)
-            spread = jnp.where(picked, spec[:, None, :], 0.0).reshape(n_chan * groups, depth).astype(jnp.bfloat16)
+            slabs = []
+            for slab in range(depth // LANES):
+                rows = [jnp.where(picked, flipped[slab, pl.ds(r * LANES + j, 1), :], 0.0) for r in range(n_chan)]
+                slabs.append(jnp.concatenate(rows, axis=0).astype(jnp.bfloat16))
+            spread = jnp.concatenate(slabs, axis=1)
             cross = jnp.dot(spread, weights[j], preferred_element_type=jnp.float32)
             for half, kept in ((0, reals), (1, imags)):
                 part = cross[:, half * 2 * n_src:(half + 1) * 2 * n_src].reshape(n_chan // 2, 2, groups, 2 * n_src)
@@ -191,8 +197,32 @@
         @pl.when(can_send(0, way))
         def _():
             src_hop(0, way).start()
-    for c in range(2, CHUNKS):
-        start_own(c)
+    def block_copy(owner, origin, target, send_sem, recv_sem):
+        block = src_out.at[pl.ds(owner * part, part), pl.ds(pl.multiple_of(origin * rows, rows), rows), :]
+        return pltpu.make_async_remote_copy(
+            src_ref=block, dst_ref=block, send_sem=send_sem, recv_sem=recv_sem,
+            device_id=(me_w, target), device_id_type=MESH)
+
+    def chip_copy(w, d):
+        return block_copy(me_r, w, lax.rem(me_r + 2 * d, n_rcv), x_send.at[w, d], x_recv.at[w, d])
+
+    def chip_arrival(w, d):
+        return block_copy(lax.rem(me_r - 2 * d + n_rcv, n_rcv), w, sibling, x_send.at[w, d], x_recv.at[w, d])
+
+    def core_copy(w, d):
+        return block_copy(lax.rem(me_r - 2 * d + n_rcv, n_rcv), w, sibling, c_send.at[w, d], c_recv.at[w, d])
+
+    def core_arrival(w, d):
+        return block_copy(lax.rem(sibling - 2 * d + n_rcv, n_rcv), w, sibling, c_send.at[w, d], c_recv.at[w, d])
+
+    def spread_block(w):
+        @pl.loop(1, n_chip)
+        def _(d):
+            chip_copy(w, d).start()
+
+        core_copy(w, 0).start()
+
+    spread_block(me_w)
     for t in range(n_win - 1):
         for way in range(2):
             @pl.when(can_receive(t, way))
@@ -203,29 +233,12 @@
             def _():
                 src_hop(t + 1, way).start()
 
-    def block_copy(owner, target, send_sem, recv_sem):
-        block = src_out.at[pl.ds(owner * part, part)]
-        return pltpu.make_async_remote_copy(
-            src_ref=block, dst_ref=block, send_sem=send_sem, recv_sem=recv_sem,
-            device_id=(me_w, target), device_id_type=MESH)
-
-    def chip_copy(d):
-        return block_copy(me_r, lax.rem(me_r + 2 * d, n_rcv), x_send.at[d], x_recv.at[d])
-
-    def core_copy(d):
-        return block_copy(lax.rem(me_r - 2 * d + n_rcv, n_rcv), sibling, c_send.at[d], c_recv.at[d])
-
-    def core_arrival(d):
-        return block_copy(lax.rem(sibling - 2 * d + n_rcv, n_rcv), sibling, c_send.at[d], c_recv.at[d])
-
-    def chip_arrival(d):
-        return block_copy(lax.rem(me_r - 2 * d + n_rcv, n_rcv), sibling, x_send.at[d], x_recv.at[d])
-
-    @pl.loop(1, n_chip)
-    def _(d):
-        chip_copy(d).start()
-
-    core_copy(0).start()
+            @pl.when(can_receive(t, way))
+            def _():
+                spread_block(me_w - (1 - 2 * way) * (t + 1))
+
+    for c in range(2, CHUNKS):
+        start_own(c)
 
     def forward(c, t):
         for way in range(2):
@@ -240,16 +253,20 @@
     for t in range(n_win - 1):
         forward(0, t)
 
-    @pl.loop(1, n_chip)
-    def _(d):
-        chip_arrival(d).wait_recv()
-        core_copy(d).start()
+    @pl.loop(0, n_win)
+    def _(w):
+        @pl.loop(1, n_chip)
+        def _(d):
+            chip_arrival(w, d).wait_recv()
+            core_copy(w, d).start()
 
     forward(1, 0)
 
-    @pl.loop(0, n_chip)
-    def _(d):
-        core_arrival(d).wait_recv()
+    @pl.loop(0, n_win)
+    def _(w):
+        @pl.loop(0, n_chip)
+        def _(d):
+            core_arrival(w, d).wait_recv()
 
     prepare_source(groups, src_out, flipped, weights)
 
@@ -280,13 +297,15 @@
 
     compute(CHUNKS - 1, False)
 
-    @pl.loop(0, n_chip)
-    def _(d):
-        core_copy(d).wait_send()
-
-    @pl.loop(1, n_chip)
-    def _(d):
-        chip_copy(d).wait_send()
+    @pl.loop(0, n_win)
+    def _(w):
+        @pl.loop(0, n_chip)
+        def _(d):
+            core_copy(w, d).wait_send()
+
+        @pl.loop(1, n_chip)
+        def _(d):
+            chip_copy(w, d).wait_send()
 
     for t in range(n_win - 1):
         for way in range(2):
@@ -325,8 +344,8 @@
             sem((n_rcv,)), sem((n_rcv,)),
             sem((2, n_win, CHUNKS)), sem((2, n_win, CHUNKS)),
             sem((2, n_win)), sem((2, n_win)),
-            sem((n_rcv,)), sem((n_rcv,)),
-            sem((n_rcv,)), sem((n_rcv,)),
+            sem((n_win, n_rcv)), sem((n_win, n_rcv)),
+            sem((n_win, n_rcv)), sem((n_win, n_rcv)),
             sem((2,)),
         ],
         compiler_params=pltpu.CompilerParams(

time: 198 us -> 169 us (0.85)
  Pallas kernels: 187 us -> 158 us
    pallas_call x1, Pallas kernels: 187 us -> 158 us  [fused(): pl.pallas_call(functools.partial(fused_kernel, n_win, n_rcv, groups, lag_...]
where the time goes in v3:
time: 169 us
  Pallas kernels  158 us (93%)
  local copies, waits for them, and re-layouts  10.3 us (6%)
    pallas_call x1, Pallas kernels, fused(): pl.pallas_call(functools.partial(fused_kernel, n_win, n_rcv, groups, lag_...  158 us
    unnamed x1, local copies, waits for them, and re-layouts  4.7 us

profile of v3, /device:TPU:0, one launch (start us, length us, event | category | flops | bytes accessed | tf_op | source)
XLA Modules:
  0.0 169.0 jit_solution(6553568768174873774)
XLA Ops:
  0.7 2.5 %reshape.3.own_ref = bf16[64,64,128]{2,1,0:T(8,128)(2,1)} reshape(bf16[64,4,2,1024]{3,2,1,0:T(2,128)(2,1)} %param.3) | data formatting | bytes 2097152 | tf_op jit(solution)/shard_map/reshape | solution.py:363
  3.2 3.1 %dynamic-slice_bitcast_fusion.table_ref = bf16[2,512,1024]{2,1,0:T(8,128)(2,1)} fusion(bf16[4,2,512,1024]{3,2,1,0:T(8,128)(2,1)} %constant.13.clone, s32[]{:T(128)S(6)} %select_n.4), kind=kLoop, calls=%fused_computation | loop fusion | bytes 4194308 | tf_op jit(solution)/shard_map/jit(dynamic_index_in_dim)/squeeze | solution.py:362
  6.3 158.0 %fused.1 = bf16[64,64,512]{2,1,0:T(8,128)(2,1)} custom-call(s32[1]{0:T(128)S(6)} %copy.5.root_ref, bf16[64,64,128]{2,1,0:T(8,128)(2,1)} %reshape.3.own_ref, bf16[2,512,1024]{2,1,0:T(8,128)(2,1)} %dynamic-slice_bitcast_fusion.table_ref), custom_call_target="tpu_custom_call" | custom-call | tf_op jit(solution)/shard_map/fused/pallas_call | solution.py:327
  164.3 4.7 %copy.6 = bf16[64,64,512]{2,1,0:T(8,128)(2,1)} copy(bf16[64,64,512]{2,1,0:T(8,128)(2,1)} %fused.1) | data formatting | bytes 8388608

commit v4 on v3

--- a/solution.py
+++ b/solution.py
@@ -13,6 +13,7 @@
 MESH = pl.DeviceIdType.MESH
 LANES = 128
 CHUNKS = 4
+HALVES = 2
 
 
 def lag_table(n_freqs, n_win, groups):
@@ -22,7 +23,8 @@
     lag = (np.arange(n_lags) - n_freqs).reshape(n_win, 1, n_lags // n_win, 1)
     angle = (2.0 * math.pi / n_lags) * ((freq * lag) % n_lags)
     table = np.concatenate([np.cos(angle), -np.sin(angle)], axis=1)
-    return table.astype(ml_dtypes.bfloat16)
+    slabs = table.reshape(n_win, 2, n_lags // n_win, groups, LANES).swapaxes(2, 3)
+    return np.ascontiguousarray(slabs).astype(ml_dtypes.bfloat16)
 
 
 def store_turned(flipped, row, block):
@@ -40,13 +42,13 @@
 def prepare_source(groups, s_ref, flipped, weights):
     n_src, depth, _ = s_ref.shape
 
-    @pl.loop(0, n_src)
+    @pl.loop(0, n_src, unroll=4)
     def _(s):
         store_turned(flipped, s, s_ref[s])
 
     first_half = lax.broadcasted_iota(jnp.int32, (1, 2 * n_src), 1) < n_src
 
-    @pl.loop(0, LANES // 2)
+    @pl.loop(0, LANES // 2, unroll=2)
     def _(jp):
         both = jnp.concatenate([load_turned(flipped, 2 * jp, n_src), load_turned(flipped, 2 * jp + 1, n_src)], axis=0).T
         crossed = pltpu.roll(both, n_src, 1)
@@ -59,7 +61,7 @@
 
 
 def turn_receivers(first, count, r_ref, flipped):
-    @pl.loop(0, count)
+    @pl.loop(0, count, unroll=4)
     def _(r):
         store_turned(flipped, r, r_ref[first + r])
 
@@ -70,7 +72,7 @@
     picked = lax.rem(lax.broadcasted_iota(jnp.int32, (groups, LANES), 1), groups) == row
     first_half = lax.broadcasted_iota(jnp.int32, (1, 1, 2 * n_src), 2) < n_src
 
-    @pl.loop(first, last)
+    @pl.loop(first, last, unroll=2)
     def _(jp):
         reals, imags = [], []
         for k in range(2):
@@ -92,18 +94,19 @@
 def lags_of(first, n_chan, lag_scale, table_ref, x_real, x_imag, out_ref):
     n_src, n_lags = out_ref.shape[1:]
 
-    @pl.loop(0, n_chan // 4)
+    @pl.loop(0, n_chan // 4, unroll=2)
     def _(q):
         real = jnp.concatenate([x_real[2 * q], x_real[2 * q + 1]], axis=1)
         imag = jnp.concatenate([x_imag[2 * q], x_imag[2 * q + 1]], axis=1)
-        lagged = jnp.dot(table_ref[0], real, preferred_element_type=jnp.float32)
-        lagged += jnp.dot(table_ref[1], imag, preferred_element_type=jnp.float32)
+        cosines, sines = (jnp.concatenate([table_ref[p, k] for k in range(table_ref.shape[1])], axis=1) for p in range(2))
+        lagged = jnp.dot(cosines, real, preferred_element_type=jnp.float32)
+        lagged += jnp.dot(sines, imag, preferred_element_type=jnp.float32)
         turned = (lagged * lag_scale).T.astype(jnp.bfloat16)
         out_ref[pl.ds(first + q * 4, 4)] = turned.reshape(4, n_src, n_lags)
 
 
 def fused_kernel(n_win, n_rcv, groups, lag_scale, root_ref, own_ref, table_ref, out_ref, recv_out, src_out, slots,
-                 flipped, weights, x_real, x_imag, sp_send, sp_recv, r_send, r_recv, z_send, z_recv, x_send, x_recv,
+                 table, flipped, weights, x_real, x_imag, sp_send, sp_recv, r_send, r_recv, z_send, z_recv, x_send, x_recv,
                  c_send, c_recv, local_sem):
     me_w = lax.axis_index("win")
     me_r = lax.axis_index("rcv")
@@ -170,6 +173,8 @@
     def _(d):
         piece_copy(d).start()
 
+    table_local = pltpu.make_async_copy(table_ref.at[me_w], table, local_sem.at[2])
+    table_local.start()
     own_local = pltpu.make_async_copy(own_ref, recv_out.at[:, pl.ds(me_w * rows, rows), :], local_sem.at[0])
     own_local.start()
     piece_local = pltpu.make_async_copy(own_ref.at[pl.ds(me_r * part, part)], slots.at[me_r], local_sem.at[1])
@@ -260,7 +265,8 @@
             chip_arrival(w, d).wait_recv()
             core_copy(w, d).start()
 
-    forward(1, 0)
+    for t in range(n_win - 1):
+        forward(1, t)
 
     @pl.loop(0, n_win)
     def _(w):
@@ -268,34 +274,26 @@
         def _(d):
             core_arrival(w, d).wait_recv()
 
+    def forward_rest(t):
+        for c in range(CHUNKS // HALVES, CHUNKS):
+            forward(c, t)
+
+    forward_rest(0)
     prepare_source(groups, src_out, flipped, weights)
-
+    forward_rest(1)
+
+    half = n_chan // HALVES
     pairs = LANES // 2
-    cuts = [pairs * t // n_win for t in range(n_win + 1)]
-
-    def compute(c, ahead):
-        turn_receivers(c * chunk, chunk, recv_out, flipped)
-        for t in range(n_win):
-            cross_part(cuts[t], cuts[t + 1], groups, chunk, flipped, weights, x_real, x_imag)
-            if ahead and t < n_win - 1:
-                forward(c + 1, t)
-        lags_of(c * chunk, chunk, lag_scale, table_ref, x_real, x_imag, out_ref)
-
-    def compute_first():
-        turn_receivers(0, chunk, recv_out, flipped)
-        for t in range(n_win):
-            cross_part(cuts[t], cuts[t + 1], groups, chunk, flipped, weights, x_real, x_imag)
-            if 0 < t < n_win - 1:
-                forward(1, t)
-        lags_of(0, chunk, lag_scale, table_ref, x_real, x_imag, out_ref)
-
-    compute_first()
-
-    @pl.loop(1, CHUNKS - 1)
-    def _(c):
-        compute(c, True)
-
-    compute(CHUNKS - 1, False)
+    turn_receivers(0, half, recv_out, flipped)
+    cross_part(0, pairs // 2, groups, half, flipped, weights, x_real, x_imag)
+    for t in range(2, n_win - 1):
+        forward_rest(t)
+    cross_part(pairs // 2, pairs, groups, half, flipped, weights, x_real, x_imag)
+    table_local.wait()
+    lags_of(0, half, lag_scale, table, x_real, x_imag, out_ref)
+    turn_receivers(half, half, recv_out, flipped)
+    cross_part(0, pairs, groups, half, flipped, weights, x_real, x_imag)
+    lags_of(half, half, lag_scale, table, x_real, x_imag, out_ref)
 
     @pl.loop(0, n_win)
     def _(w):
@@ -319,9 +317,9 @@
 def fused(root, own, table, n_win, n_rcv, lag_scale, groups):
     n_chan, rows, lanes = own.shape
     part = n_chan // n_rcv
-    chunk = n_chan // CHUNKS
+    half = n_chan // HALVES
     depth = n_win * rows
-    n_lags, n_freqs = table.shape[1:]
+    n_lags, n_freqs = table.shape[3], table.shape[2] * lanes
     bf16 = own.dtype
     sem = pltpu.SemaphoreType.DMA
     return pl.pallas_call(
@@ -330,23 +328,24 @@
         in_specs=[
             pl.BlockSpec(memory_space=pltpu.SMEM),
             pl.BlockSpec(memory_space=pl.ANY),
-            pl.BlockSpec(memory_space=pltpu.VMEM),
+            pl.BlockSpec(memory_space=pl.ANY),
         ],
         out_specs=pl.BlockSpec(memory_space=pltpu.VMEM),
         scratch_shapes=[
             pltpu.VMEM((n_chan, depth, lanes), bf16),
             pltpu.VMEM((n_chan, depth, lanes), bf16),
             pltpu.VMEM((n_rcv, part, rows, lanes), bf16),
+            pltpu.VMEM(table.shape[1:], bf16),
             pltpu.VMEM((depth // LANES, n_chan * lanes, LANES), jnp.float32),
             pltpu.VMEM((lanes, depth, 4 * n_chan), bf16),
-            pltpu.VMEM((chunk // 2, n_freqs, 2 * n_chan), bf16),
-            pltpu.VMEM((chunk // 2, n_freqs, 2 * n_chan), bf16),
+            pltpu.VMEM((half // 2, n_freqs, 2 * n_chan), bf16),
+            pltpu.VMEM((half // 2, n_freqs, 2 * n_chan), bf16),
             sem((n_rcv,)), sem((n_rcv,)),
             sem((2, n_win, CHUNKS)), sem((2, n_win, CHUNKS)),
             sem((2, n_win)), sem((2, n_win)),
             sem((n_win, n_rcv)), sem((n_win, n_rcv)),
             sem((n_win, n_rcv)), sem((n_win, n_rcv)),
-            sem((2,)),
+            sem((3,)),
         ],
         compiler_params=pltpu.CompilerParams(
             collective_id=0, has_side_effects=True, vmem_limit_bytes=56 << 20),
@@ -358,8 +357,7 @@
     n_chan, n_time, parts, n_freqs = spectra.shape
     groups = n_freqs // LANES
     lag_scale = 1.0 / math.sqrt(2 * n_freqs * n_time * n_win)
-    tables = jnp.asarray(lag_table(n_freqs, n_win, groups))
-    table = lax.dynamic_index_in_dim(tables, lax.axis_index("win"), 0, keepdims=False)
+    table = jnp.asarray(lag_table(n_freqs, n_win, groups))
     own = spectra.reshape(n_chan, n_time * parts * groups, LANES)
     return fused(source_block, own, table, n_win, n_rcv, lag_scale, groups)
 

time: 169 us -> 128 us (0.76)
  Pallas kernels: 158 us -> 120 us
  local copies, waits for them, and re-layouts: 10.3 us -> 7.21 us
    pallas_call x1, Pallas kernels: 158 us -> 120 us  [fused(): pl.pallas_call(functools.partial(fused_kernel, n_win, n_rcv, groups, lag_...]
    squeeze x1 -> x0, local copies, waits for them, and re-layouts: 3.08 us -> none  [body(): lax.dynamic_index_in_dim(tables, lax.axis_index('win'), 0, keepdims=False)]
where the time goes in v4:
time: 128 us
  Pallas kernels  120 us (94%)
  local copies, waits for them, and re-layouts  7.21 us (6%)
    pallas_call x1, Pallas kernels, fused(): pl.pallas_call(functools.partial(fused_kernel, n_win, n_rcv, groups, lag_...  120 us
    unnamed x1, local copies, waits for them, and re-layouts  4.7 us

profile of v4, /device:TPU:0, one launch (start us, length us, event | category | flops | bytes accessed | tf_op | source)
XLA Modules:
  0.0 127.6 jit_solution(1456003064939887052)
XLA Ops:
  0.7 2.5 %reshape.3.own_ref = bf16[64,64,128]{2,1,0:T(8,128)(2,1)} reshape(bf16[64,4,2,1024]{3,2,1,0:T(2,128)(2,1)} %param.3) | data formatting | bytes 2097152 | tf_op jit(solution)/shard_map/reshape | solution.py:361
  3.2 119.8 %fused.1 = bf16[64,64,512]{2,1,0:T(8,128)(2,1)} custom-call(s32[1]{0:T(128)S(6)} %copy.5.root_ref, bf16[64,64,128]{2,1,0:T(8,128)(2,1)} %reshape.3.own_ref, bf16[4,2,8,512,128]{4,3,2,1,0:T(8,128)(2,1)} %constant.2.clone.table_ref), custom_call_target="tpu_custom_call" | custom-call | tf_op jit(solution)/shard_map/fused/pallas_call | solution.py:325
  122.9 4.7 %copy.6 = bf16[64,64,512]{2,1,0:T(8,128)(2,1)} copy(bf16[64,64,512]{2,1,0:T(8,128)(2,1)} %fused.1) | data formatting | bytes 8388608

commit v5 on v4

--- a/solution.py
+++ b/solution.py
@@ -39,16 +39,11 @@
     return jnp.concatenate(slabs, axis=1)
 
 
-def prepare_source(groups, s_ref, flipped, weights):
-    n_src, depth, _ = s_ref.shape
-
-    @pl.loop(0, n_src, unroll=4)
-    def _(s):
-        store_turned(flipped, s, s_ref[s])
-
+def prepare_source(groups, n_src, flipped, weights):
+    depth = weights.shape[1]
     first_half = lax.broadcasted_iota(jnp.int32, (1, 2 * n_src), 1) < n_src
 
-    @pl.loop(0, LANES // 2, unroll=2)
+    @pl.loop(0, LANES // 2, unroll=4)
     def _(jp):
         both = jnp.concatenate([load_turned(flipped, 2 * jp, n_src), load_turned(flipped, 2 * jp + 1, n_src)], axis=0).T
         crossed = pltpu.roll(both, n_src, 1)
@@ -60,10 +55,10 @@
             weights[2 * jp + k, :, 2 * n_src:] = imag.astype(jnp.bfloat16)
 
 
-def turn_receivers(first, count, r_ref, flipped):
-    @pl.loop(0, count, unroll=4)
+def turn(first, count, row, ref, flipped):
+    @pl.loop(0, count, unroll=min(count, 8))
     def _(r):
-        store_turned(flipped, r, r_ref[first + r])
+        store_turned(flipped, row + r, ref[first + r])
 
 
 def cross_part(first, last, groups, n_chan, flipped, weights, x_real, x_imag):
@@ -72,7 +67,7 @@
     picked = lax.rem(lax.broadcasted_iota(jnp.int32, (groups, LANES), 1), groups) == row
     first_half = lax.broadcasted_iota(jnp.int32, (1, 1, 2 * n_src), 2) < n_src
 
-    @pl.loop(first, last, unroll=2)
+    @pl.loop(first, last, unroll=4)
     def _(jp):
         reals, imags = [], []
         for k in range(2):
@@ -106,7 +101,7 @@
 
 
 def fused_kernel(n_win, n_rcv, groups, lag_scale, root_ref, own_ref, table_ref, out_ref, recv_out, src_out, slots,
-                 table, flipped, weights, x_real, x_imag, sp_send, sp_recv, r_send, r_recv, z_send, z_recv, x_send, x_recv,
+                 table, result, flipped, spread_rows, weights, x_real, x_imag, sp_send, sp_recv, r_send, r_recv, z_send, z_recv, x_send, x_recv,
                  c_send, c_recv, local_sem):
     me_w = lax.axis_index("win")
     me_r = lax.axis_index("rcv")
@@ -268,32 +263,53 @@
     for t in range(n_win - 1):
         forward(1, t)
 
+    def forward_rest(t):
+        for c in range(CHUNKS // HALVES, CHUNKS):
+            forward(c, t)
+
+    def turn_source(owner):
+        turn(owner * part, part, owner * part, src_out, flipped)
+
+    half = n_chan // HALVES
+    turn(0, half, 0, recv_out, spread_rows)
+
+    @pl.loop(0, n_chip)
+    def _(d):
+        turn_source(lax.rem(me_r - 2 * d + n_rcv, n_rcv))
+
     @pl.loop(0, n_win)
     def _(w):
         @pl.loop(0, n_chip)
         def _(d):
             core_arrival(w, d).wait_recv()
 
-    def forward_rest(t):
-        for c in range(CHUNKS // HALVES, CHUNKS):
-            forward(c, t)
-
     forward_rest(0)
-    prepare_source(groups, src_out, flipped, weights)
+
+    @pl.loop(0, n_chip)
+    def _(d):
+        turn_source(lax.rem(sibling - 2 * d + n_rcv, n_rcv))
+
+    prepare_source(groups, n_chan, flipped, weights)
     forward_rest(1)
 
-    half = n_chan // HALVES
+    def result_copy(first, which):
+        rows_of = pl.ds(first, half)
+        return pltpu.make_async_copy(result.at[rows_of], out_ref.at[rows_of], local_sem.at[3 + which])
+
     pairs = LANES // 2
-    turn_receivers(0, half, recv_out, flipped)
-    cross_part(0, pairs // 2, groups, half, flipped, weights, x_real, x_imag)
+    cross_part(0, pairs // 2, groups, half, spread_rows, weights, x_real, x_imag)
     for t in range(2, n_win - 1):
         forward_rest(t)
-    cross_part(pairs // 2, pairs, groups, half, flipped, weights, x_real, x_imag)
+    cross_part(pairs // 2, pairs, groups, half, spread_rows, weights, x_real, x_imag)
     table_local.wait()
-    lags_of(0, half, lag_scale, table, x_real, x_imag, out_ref)
-    turn_receivers(half, half, recv_out, flipped)
-    cross_part(0, pairs, groups, half, flipped, weights, x_real, x_imag)
-    lags_of(half, half, lag_scale, table, x_real, x_imag, out_ref)
+    lags_of(0, half, lag_scale, table, x_real, x_imag, result)
+    result_copy(0, 0).start()
+    turn(half, half, 0, recv_out, spread_rows)
+    cross_part(0, pairs, groups, half, spread_rows, weights, x_real, x_imag)
+    lags_of(half, half, lag_scale, table, x_real, x_imag, result)
+    result_copy(half, 1).start()
+    result_copy(0, 0).wait()
+    result_copy(half, 1).wait()
 
     @pl.loop(0, n_win)
     def _(w):
@@ -330,13 +346,15 @@
             pl.BlockSpec(memory_space=pl.ANY),
             pl.BlockSpec(memory_space=pl.ANY),
         ],
-        out_specs=pl.BlockSpec(memory_space=pltpu.VMEM),
+        out_specs=pl.BlockSpec(memory_space=pl.ANY),
         scratch_shapes=[
             pltpu.VMEM((n_chan, depth, lanes), bf16),
             pltpu.VMEM((n_chan, depth, lanes), bf16),
             pltpu.VMEM((n_rcv, part, rows, lanes), bf16),
             pltpu.VMEM(table.shape[1:], bf16),
+            pltpu.VMEM((n_chan, n_chan, n_lags), bf16),
             pltpu.VMEM((depth // LANES, n_chan * lanes, LANES), jnp.float32),
+            pltpu.VMEM((depth // LANES, half * lanes, LANES), jnp.float32),
             pltpu.VMEM((lanes, depth, 4 * n_chan), bf16),
             pltpu.VMEM((half // 2, n_freqs, 2 * n_chan), bf16),
             pltpu.VMEM((half // 2, n_freqs, 2 * n_chan), bf16),
@@ -345,10 +363,10 @@
             sem((2, n_win)), sem((2, n_win)),
             sem((n_win, n_rcv)), sem((n_win, n_rcv)),
             sem((n_win, n_rcv)), sem((n_win, n_rcv)),
-            sem((3,)),
+            sem((5,)),
         ],
         compiler_params=pltpu.CompilerParams(
-            collective_id=0, has_side_effects=True, vmem_limit_bytes=56 << 20),
+            collective_id=0, has_side_effects=True, vmem_limit_bytes=58 << 20),
         name="fused",
     )(root, own, table)
 

time: 128 us -> 123 us (0.961)
  Pallas kernels: 120 us -> 115 us
    pallas_call x1, Pallas kernels: 120 us -> 115 us  [fused(): pl.pallas_call(functools.partial(fused_kernel, n_win, n_rcv, groups, lag_...]
where the time goes in v5:
time: 123 us
  Pallas kernels  115 us (93%)
  local copies, waits for them, and re-layouts  7.21 us (6%)
    pallas_call x1, Pallas kernels, fused(): pl.pallas_call(functools.partial(fused_kernel, n_win, n_rcv, groups, lag_...  115 us
    unnamed x1, local copies, waits for them, and re-layouts  4.7 us
    reshape x1, local copies, waits for them, and re-layouts, body(): own = spectra.reshape(n_chan, n_time * parts * groups, LANES)  2.52 us

profile of v5, /device:TPU:0, one launch (start us, length us, event | category | flops | bytes accessed | tf_op | source)
XLA Modules:
  0.0 122.6 jit_solution(8704445530733636816)
XLA Ops:
  0.7 2.5 %reshape.3.own_ref = bf16[64,64,128]{2,1,0:T(8,128)(2,1)} reshape(bf16[64,4,2,1024]{3,2,1,0:T(2,128)(2,1)} %param.3) | data formatting | bytes 2097152 | tf_op jit(solution)/shard_map/reshape | solution.py:379
  3.2 114.7 %fused.1 = bf16[64,64,512]{2,1,0:T(8,128)(2,1)} custom-call(s32[1]{0:T(128)S(6)} %copy.5.root_ref, bf16[64,64,128]{2,1,0:T(8,128)(2,1)} %reshape.3.own_ref, bf16[4,2,8,512,128]{4,3,2,1,0:T(8,128)(2,1)} %constant.2.clone.table_ref), custom_call_target="tpu_custom_call" | custom-call | tf_op jit(solution)/shard_map/fused/pallas_call | solution.py:341
  117.9 4.7 %copy.6 = bf16[64,64,512]{2,1,0:T(8,128)(2,1)} copy(bf16[64,64,512]{2,1,0:T(8,128)(2,1)} %fused.1) | data formatting | bytes 8388608

commit v6 on v5

--- a/solution.py
+++ b/solution.py
@@ -237,9 +237,6 @@
             def _():
                 spread_block(me_w - (1 - 2 * way) * (t + 1))
 
-    for c in range(2, CHUNKS):
-        start_own(c)
-
     def forward(c, t):
         for way in range(2):
             @pl.when(can_receive(t, way))
@@ -250,8 +247,11 @@
             def _():
                 recv_hop(c, t + 1, way).start()
 
-    for t in range(n_win - 1):
-        forward(0, t)
+    def forward_first(t):
+        for c in range(CHUNKS // HALVES):
+            forward(c, t)
+
+    forward_first(0)
 
     @pl.loop(0, n_win)
     def _(w):
@@ -260,8 +260,10 @@
             chip_arrival(w, d).wait_recv()
             core_copy(w, d).start()
 
-    for t in range(n_win - 1):
-        forward(1, t)
+    for t in range(1, n_win - 2):
+        forward_first(t)
+    for c in range(CHUNKS // HALVES, CHUNKS):
+        start_own(c)
 
     def forward_rest(t):
         for c in range(CHUNKS // HALVES, CHUNKS):
@@ -271,8 +273,6 @@
         turn(owner * part, part, owner * part, src_out, flipped)
 
     half = n_chan // HALVES
-    turn(0, half, 0, recv_out, spread_rows)
-
     @pl.loop(0, n_chip)
     def _(d):
         turn_source(lax.rem(me_r - 2 * d + n_rcv, n_rcv))
@@ -283,14 +283,14 @@
         def _(d):
             core_arrival(w, d).wait_recv()
 
+    @pl.loop(0, n_chip)
+    def _(d):
+        turn_source(lax.rem(sibling - 2 * d + n_rcv, n_rcv))
+
+    prepare_source(groups, n_chan, flipped, weights)
+    forward_first(n_win - 2)
     forward_rest(0)
-
-    @pl.loop(0, n_chip)
-    def _(d):
-        turn_source(lax.rem(sibling - 2 * d + n_rcv, n_rcv))
-
-    prepare_source(groups, n_chan, flipped, weights)
-    forward_rest(1)
+    turn(0, half, 0, recv_out, spread_rows)
 
     def result_copy(first, which):
         rows_of = pl.ds(first, half)
@@ -298,12 +298,13 @@
 
     pairs = LANES // 2
     cross_part(0, pairs // 2, groups, half, spread_rows, weights, x_real, x_imag)
-    for t in range(2, n_win - 1):
+    for t in range(1, n_win - 2):
         forward_rest(t)
     cross_part(pairs // 2, pairs, groups, half, spread_rows, weights, x_real, x_imag)
     table_local.wait()
     lags_of(0, half, lag_scale, table, x_real, x_imag, result)
     result_copy(0, 0).start()
+    forward_rest(n_win - 2)
     turn(half, half, 0, recv_out, spread_rows)
     cross_part(0, pairs, groups, half, spread_rows, weights, x_real, x_imag)
     lags_of(half, half, lag_scale, table, x_real, x_imag, result)

time: 123 us -> 114 us (0.927)
  Pallas kernels: 115 us -> 106 us
    pallas_call x1, Pallas kernels: 115 us -> 106 us  [fused(): pl.pallas_call(functools.partial(fused_kernel, n_win, n_rcv, groups, lag_...]
where the time goes in v6:
time: 114 us
  Pallas kernels  106 us (93%)
  local copies, waits for them, and re-layouts  7.21 us (6%)
    pallas_call x1, Pallas kernels, fused(): pl.pallas_call(functools.partial(fused_kernel, n_win, n_rcv, groups, lag_...  106 us
    unnamed x1, local copies, waits for them, and re-layouts  4.7 us
    reshape x1, local copies, waits for them, and re-layouts, body(): own = spectra.reshape(n_chan, n_time * parts * groups, LANES)  2.52 us

profile of v6, /device:TPU:0, one launch (start us, length us, event | category | flops | bytes accessed | tf_op | source)
XLA Modules:
  0.0 113.6 jit_solution(2951475638257651182)
XLA Ops:
  0.7 2.5 %reshape.3.own_ref = bf16[64,64,128]{2,1,0:T(8,128)(2,1)} reshape(bf16[64,4,2,1024]{3,2,1,0:T(2,128)(2,1)} %param.3) | data formatting | bytes 2097152 | tf_op jit(solution)/shard_map/reshape | solution.py:380
  3.2 105.7 %fused.1 = bf16[64,64,512]{2,1,0:T(8,128)(2,1)} custom-call(s32[1]{0:T(128)S(6)} %copy.5.root_ref, bf16[64,64,128]{2,1,0:T(8,128)(2,1)} %reshape.3.own_ref, bf16[4,2,8,512,128]{4,3,2,1,0:T(8,128)(2,1)} %constant.2.clone.table_ref), custom_call_target="tpu_custom_call" | custom-call | tf_op jit(solution)/shard_map/fused/pallas_call | solution.py:342
  108.9 4.7 %copy.6 = bf16[64,64,512]{2,1,0:T(8,128)(2,1)} copy(bf16[64,64,512]{2,1,0:T(8,128)(2,1)} %fused.1) | data formatting | bytes 8388608
